TPU v7x, 32 devices: a whole 2x2x4 slice. The times are simulated.
32 devices in a mesh: head: 4 (over x, core), blk: 8 (over z, y).
Axes of the slice: x: 2, y: 2, z: 4, core: 2. Of those that a mesh axis runs over, the one named last changes fastest.
Arguments:
- inputs: bfloat16 [1536, 1, 3072], P('blk', None, 'head'), may hold values from -17.5 to 17.5
- out_grad: bfloat16 [1536, 1, 3072], P('blk', None, 'head'), may hold values from -6 to 6
- qkv_weight: bfloat16 [3072, 3, 1536], P(None, None, 'head'), may hold values from -0.108253175 to 0.108253175
- out_weight: bfloat16 [3072, 1536], P(None, 'head'), may hold values from -0.15625 to 0.15625
- text_keys: bfloat16 [256, 1, 1536], P(None, None, 'head'), may hold values from -6 to 6
- text_values: bfloat16 [256, 1, 1536], P(None, None, 'head'), may hold values from -6 to 6
- text_mask: int32 [256, 1], replicated, may hold values 0 or 1
Outputs:
- grad_inputs: bfloat16 [1536, 1, 3072], P('blk', None, 'head')
- grad_qkv_weight: float32 [3072, 3, 1536], P('blk', None, 'head')
- grad_out_weight: float32 [3072, 1536], P('blk', 'head')
- grad_text_keys: float32 [256, 1, 1536], P('blk', None, 'head')
- grad_text_values: float32 [256, 1, 1536], P('blk', None, 'head')
All inputs are finite; a program needn't handle non-finite values.
Results may differ from a plain program's by a relative error of at most 0.034.
Values may be sent and summed in bfloat16 or wider, within the bound.
A program may use at most 128 MiB of HBM per device.

v0:
```python
import jax
import jax.numpy as jnp
from jax import lax
from jax.sharding import PartitionSpec as P

HD = 128


masked_fill = -1000000000.0


def masked_logits(query_heads, key_rows, valid_rows, score_scale):
    logits = (
        jnp.einsum("vsne,jsne->snvj", query_heads, key_rows, preferred_element_type=jnp.float32)
        * score_scale
    )
    if valid_rows is not None:
        logits = jnp.where(valid_rows.T[:, None, None, :], logits, masked_fill)
    return logits


def attend_block(softmax_state, query_heads, key_rows, value_rows, valid_rows, score_scale):
    running_max, running_sum, running_acc = softmax_state
    logits = masked_logits(query_heads, key_rows, valid_rows, score_scale)
    new_max = jnp.maximum(running_max, jnp.max(logits, axis=-1))
    factor = jnp.exp(running_max - new_max)
    weights = jnp.exp(logits - new_max[..., None])
    new_sum = running_sum * factor + jnp.sum(weights, axis=-1)
    update = jnp.einsum(
        "snvj,jsne->snve",
        weights.astype(jnp.bfloat16),
        value_rows,
        preferred_element_type=jnp.float32,
    )
    return (new_max, new_sum, running_acc * factor[..., None] + update)


def grad_block(
    query_heads, grad_heads, key_rows, value_rows, valid_rows, log_total, row_dot, score_scale
):
    logits = masked_logits(query_heads, key_rows, valid_rows, score_scale)
    probabilities = jnp.exp(logits - log_total[..., None])
    grad_values = jnp.einsum(
        "snvj,vsne->jsne",
        probabilities.astype(jnp.bfloat16),
        grad_heads,
        preferred_element_type=jnp.float32,
    )
    grad_probs = jnp.einsum(
        "vsne,jsne->snvj", grad_heads, value_rows, preferred_element_type=jnp.float32
    )
    grad_logits = (probabilities * (grad_probs - row_dot[..., None]) * score_scale).astype(
        jnp.bfloat16
    )
    grad_queries = jnp.einsum(
        "snvj,jsne->vsne", grad_logits, key_rows, preferred_element_type=jnp.float32
    )
    grad_keys = jnp.einsum(
        "snvj,vsne->jsne", grad_logits, query_heads, preferred_element_type=jnp.float32
    )
    return (grad_queries, jnp.stack([grad_keys, grad_values], axis=2))


def key_blocks(full_kv, shard_rows, shards, seq_count, head_count, head_dim):
    group_size = 1
    while group_size * shard_rows < 512 and group_size < shards:
        group_size = group_size * 2
    return full_kv.reshape(
        shards // group_size, group_size * shard_rows, seq_count, 2, head_count, head_dim
    )


def per_device(inputs, out_grad, qkv_weight, out_weight, text_keys, text_values, text_mask):
    full_in, full_grad = (
        lax.all_gather(inputs, "head", axis=2, tiled=True),
        lax.all_gather(out_grad, "head", axis=2, tiled=True),
    )
    shard_rows = inputs.shape[0]
    seq_count = inputs.shape[1]
    local_width = qkv_weight.shape[2]
    head_dim = HD
    head_count = local_width // head_dim
    score_scale = head_dim ** (-0.5)
    shards = lax.axis_size("blk")
    projected = jnp.einsum(
        "vsd,dch->vsch", full_in, qkv_weight, preferred_element_type=jnp.float32
    ).astype(jnp.bfloat16)
    grad_attn = jnp.einsum(
        "vsd,dh->vsh", full_grad, out_weight, preferred_element_type=jnp.float32
    ).astype(jnp.bfloat16)
    query_heads = projected[:, :, 0].reshape(shard_rows, seq_count, head_count, head_dim)
    grad_heads = grad_attn.reshape(shard_rows, seq_count, head_count, head_dim)
    kv_local = projected[:, :, 1:]
    text_rows = text_keys.shape[0]
    valid_text = text_mask == 1
    text_key_heads = text_keys.reshape(text_rows, seq_count, head_count, head_dim)
    text_value_heads = text_values.reshape(text_rows, seq_count, head_count, head_dim)
    start_state = (
        jnp.full((seq_count, head_count, shard_rows), -1e30, jnp.float32),
        jnp.zeros((seq_count, head_count, shard_rows), jnp.float32),
        jnp.zeros((seq_count, head_count, shard_rows, head_dim), jnp.float32),
    )
    softmax_state = attend_block(
        start_state, query_heads, text_key_heads, text_value_heads, valid_text, score_scale
    )
    kv_piece = lax.all_gather(kv_local, "blk", axis=0, tiled=True)
    key_slice = kv_piece.reshape(kv_piece.shape[0], seq_count, 2, head_count, head_dim)
    softmax_state = attend_block(
        softmax_state, query_heads, key_slice[:, :, 0], key_slice[:, :, 1], None, score_scale
    )
    run_max, run_sum, run_acc = softmax_state
    out_heads = jnp.transpose(run_acc / run_sum[..., None], (2, 0, 1, 3)).astype(jnp.bfloat16)
    attn_out = out_heads.reshape(shard_rows, seq_count, local_width)
    log_total = run_max + jnp.log(run_sum)
    row_dot = jnp.transpose(
        jnp.sum(grad_heads.astype(jnp.float32) * out_heads.astype(jnp.float32), axis=-1), (1, 2, 0)
    )
    text_query_grads, text_terms = grad_block(
        query_heads,
        grad_heads,
        text_key_heads,
        text_value_heads,
        valid_text,
        log_total,
        row_dot,
        score_scale,
    )
    text_sums = lax.psum_scatter(
        text_terms.reshape(text_rows, seq_count, 2, local_width).astype(jnp.bfloat16),
        "blk",
        scatter_dimension=0,
        tiled=True,
    ).astype(jnp.float32)
    full_kv = lax.all_gather(kv_local, "blk", axis=0, tiled=True)
    blocks = key_blocks(full_kv, shard_rows, shards, seq_count, head_count, head_dim)

    def backward_step(running, kv_block):
        partial_value, key_term = grad_block(
            query_heads,
            grad_heads,
            kv_block[:, :, 0],
            kv_block[:, :, 1],
            None,
            log_total,
            row_dot,
            score_scale,
        )
        return (running + partial_value, key_term)

    query_grads, key_terms = lax.scan(backward_step, text_query_grads, blocks)
    key_terms = key_terms.reshape(full_kv.shape[0], seq_count, 2, local_width)
    kv_grads = lax.psum_scatter(
        key_terms.astype(jnp.bfloat16), "blk", scatter_dimension=0, tiled=True
    )
    grad_projected = jnp.concatenate(
        [query_grads.astype(jnp.bfloat16).reshape(shard_rows, seq_count, 1, local_width), kv_grads],
        axis=2,
    )
    input_terms = jnp.einsum(
        "vsch,dch->vsd", grad_projected, qkv_weight, preferred_element_type=jnp.float32
    )
    grad_inputs = lax.psum_scatter(
        input_terms.astype(jnp.bfloat16), "head", scatter_dimension=2, tiled=True
    )
    qkv_part = jnp.einsum(
        "vsd,vsch->dch", full_in, grad_projected, preferred_element_type=jnp.float32
    )
    out_part = jnp.einsum("vsd,vsh->dh", full_grad, attn_out, preferred_element_type=jnp.float32)
    weight_grads = lax.psum_scatter(
        jnp.concatenate([qkv_part, out_part[:, None]], axis=1).astype(jnp.bfloat16),
        "blk",
        scatter_dimension=0,
        tiled=True,
    ).astype(jnp.float32)
    return (
        grad_inputs,
        weight_grads[:, :3],
        weight_grads[:, 3],
        text_sums[:, :, 0],
        text_sums[:, :, 1],
    )


def solution(mesh):
    return jax.shard_map(
        per_device,
        mesh=mesh,
        in_specs=(
            P("blk", None, "head"),
            P("blk", None, "head"),
            P(None, None, "head"),
            P(None, "head"),
            P(None, None, "head"),
            P(None, None, "head"),
            P(),
        ),
        out_specs=(
            P("blk", None, "head"),
            P("blk", None, "head"),
            P("blk", "head"),
            P("blk", None, "head"),
            P("blk", None, "head"),
        ),
        check_vma=False,
    )
```

profile of v0, /device:TPU:0, one launch (start us, length us, event | category | flops | bytes accessed | tf_op | source)
XLA Modules:
  0.0 493.1 jit_solution(9879155517103910533)
XLA Ops:
  8.7 21.0 %all-gather.4.cloned.1.call-done = bf16[192,1,3072]{2,0,1:T(8,128)(2,1)} async-done(((bf16[192,1,768]{2,0,1:T(8,128)(2,1)}), bf16[192,1,3072]{2,0,1:T(8,128)(2,1)}) %all-gather.4.cloned.1.call-update) | async-done | bytes 1179664 | tf_op jit(solution)/shard_map/all_gather | solution.py:75
  29.8 5.1 %fusion.19 = bf16[192,1,3,384]{3,0,2,1:T(8,128)(2,1)S(1)} fusion(bf16[3072,3,384]{2,0,1:T(8,128)(2,1)} %param.11, bf16[192,1,3072]{2,0,1:T(8,128)(2,1)} %all-gather.4.cloned.1.call-done), kind=kOutput, calls=%fused_computation.36 | convolution fusion | flops 1359175680 | bytes 8699904 | tf_op jit(solution)/shard_map/vsd,dch->vsch/dot_general | solution.py:85
  38.5 10.3 %all-gather.8.cloned.1.call-done = bf16[192,1,3072]{2,0,1:T(8,128)(2,1)} async-done(((bf16[192,1,768]{2,0,1:T(8,128)(2,1)}), bf16[192,1,3072]{2,0,1:T(8,128)(2,1)}) %all-gather.8.cloned.1.call-update) | async-done | bytes 1179664 | tf_op jit(solution)/shard_map/all_gather | solution.py:76
  48.8 2.0 fusion.29
  51.3 52.4 %all-gather.6.cloned.1.call-done = bf16[1536,1,2,384]{3,0,2,1:T(8,128)(2,1)} async-done(((bf16[192,1,2,384]{3,0,2,1:T(8,128)(2,1)}), bf16[1536,1,2,384]{3,0,2,1:T(8,128)(2,1)}) %all-gather.6.cloned.1.call-update) | async-done | bytes 2359312 | tf_op jit(solution)/shard_map/all_gather | solution.py:106
  103.7 4.3 copy.63
  108.0 2.0 fusion.68
  112.4 7.0 %reshape.395 = bf16[2,768,1,2,3,128]{5,4,1,0,3,2:T(4,128)(2,1)} reshape(bf16[1536,1,2,384]{3,0,2,1:T(8,128)(2,1)} %all-gather.6.cloned.1.call-done) | data formatting | bytes 4718592 | tf_op jit(solution)/shard_map/reshape | solution.py:68
  119.5 4.0 copy.74
  125.3 12.0 %while.12 = (s32[]{:T(128)}, f32[192,1,3,128]{3,0,2,1:T(8,128)S(1)}, bf16[2,768,1,2,3,128]{5,1,4,3,2,0:T(8,128)(2,1)}, bf16[2,768,1,2,3,128]{5,1,4,3,2,0:T(8,128...) while((s32[]{:T(128)}, ...), condition=%wide.region_6.7_spmd, body=%wide.region_5.6_spmd.sunk | while | flops 571760640 | bytes 35692708 | solution.py:150
  137.3 5.3 %copy.93 = bf16[2,768,1,2,3,128]{5,4,1,0,3,2:T(4,128)(2,1)} copy(bf16[2,768,1,2,3,128]{5,1,4,3,2,0:T(8,128)(2,1)} %get-tuple-element.49) | data formatting | bytes 4718592 | tf_op jit(solution)/shard_map/convert_element_type | solution.py:153
  142.7 7.1 %reshape.396 = bf16[1536,1,2,384]{3,0,2,1:T(8,128)(2,1)} reshape(bf16[2,768,1,2,3,128]{5,4,1,0,3,2:T(4,128)(2,1)} %copy.93) | data formatting | bytes 4718592 | tf_op jit(solution)/shard_map/convert_element_type | solution.py:153
  153.4 1.6 pad_maximum_fusion.1
  155.1 2.3 fusion.7
  157.4 60.1 %reduce-scatter.6.cloned.1.call-done = bf16[192,1,2,384]{3,0,2,1:T(8,128)(2,1)} async-done(((bf16[1536,1,2,384]{3,0,2,1:T(8,128)(2,1)}), bf16[192,1,2,384]{3,0,2,1:T(8,128)(2,1)}) %reduce-scatter.6.cloned.1.call-update) | async-done | bytes 294928 | tf_op jit(solution)/shard_map/reduce_scatter | solution.py:152
  217.5 5.9 %convert_bitcast_fusion = bf16[3072,3,384]{0,2,1:T(8,128)(2,1)} fusion(bf16[192,1,3072]{2,0,1:T(8,128)(2,1)S(1)} %copy-done.7, bf16[192,1,2,384]{3,0,2,1:T(8,128)(2,1)} %reduce-scatter.6.cloned.1.call-done, bf16[192,1,1,384]{3,0,2,1:T(8,128)(2,1)} %reshape.390), kind=kOutput, calls=%fused_computation.17 | convolution fusion | flops 1362714624 | bytes 8699904 | tf_op jit(solution)/shard_map/vsd,vsch->dch/dot_general | solution.py:165
  223.4 7.5 %pad_maximum_fusion = bf16[3072,4,384]{0,2,1:T(8,128)(2,1)} fusion(bf16[3072,1,384]{0,2,1:T(8,128)(2,1)S(1)} %fusion.7, bf16[3072,3,384]{0,2,1:T(8,128)(2,1)} %convert_bitcast_fusion), kind=kLoop, calls=%fused_computation.16 | loop fusion | flops 4718592 | bytes 18874368 | tf_op jit(solution)/shard_map/concatenate | solution.py:170
  231.0 12.8 %copy.97 = bf16[3072,1536]{1,0:T(8,128)(2,1)} copy(bf16[3072,1536]{0,1:T(8,128)(2,1)} %bitcast.245) | data formatting | bytes 18874368
  244.8 6.5 %fusion.9 = bf16[192,1,3072]{2,0,1:T(8,128)(2,1)} fusion(bf16[3072,3,384]{2,0,1:T(8,128)(2,1)} %param.11, bf16[192,1,2,384]{3,0,2,1:T(8,128)(2,1)S(1)} %copy-done.11, bf16[192,1,1,384]{3,0,2,1:T(8,128)(2,1)S(1)} %copy-done.9), kind=kOutput, calls=%fused_computation.22 | convolution fusion | flops 1359765504 | bytes 8699904 | tf_op jit(solution)/shard_map/vsch,dch->vsd/dot_general | solution.py:159
  252.6 39.1 %all-reduce.3.cloned.1.call-done = bf16[256,1,2,384]{3,2,1,0:T(2,128)(2,1)} async-done(((bf16[256,1,2,384]{3,2,1,0:T(2,128)(2,1)}), bf16[256,1,2,384]{3,2,1,0:T(2,128)(2,1)}) %all-reduce.3.cloned.1.call-update) | async-done | bytes 393232
  293.2 164.9 %reduce-scatter.10.cloned.1.call-done = bf16[384,1536]{1,0:T(8,128)(2,1)} async-done(((bf16[3072,1536]{1,0:T(8,128)(2,1)}), bf16[384,1536]{1,0:T(8,128)(2,1)}) %reduce-scatter.10.cloned.1.call-update) | async-done | bytes 1179664
  458.1 1.7 copy.98
  462.7 2.8 copy.85
  467.7 18.5 %reduce-scatter.8.cloned.1.call-done = bf16[192,1,768]{2,0,1:T(8,128)(2,1)} async-done(((bf16[192,1,3072]{2,0,1:T(8,128)(2,1)}), bf16[192,1,768]{2,0,1:T(8,128)(2,1)}) %reduce-scatter.8.cloned.1.call-update) | async-done | bytes 294928 | tf_op jit(solution)/shard_map/reduce_scatter | solution.py:162
  (100 shorter events, 33.5 us)
Async XLA Ops:
  7.2 41.7 %copy-start = (bf16[3072,384]{1,0:T(8,128)(2,1)S(1)}, bf16[3072,384]{1,0:T(8,128)(2,1)}, u32[]{:S(2)}) copy-start(bf16[3072,384]{1,0:T(8,128)(2,1)} %param.12) | copy-start | bytes 7077892
  7.2 22.6 %all-gather.4.cloned.1.call-start = ((), (), s32[]{:S(2)}) async-start(), calls=%async_computation.3 | async-start | bytes 1474560 | tf_op jit(solution)/shard_map/all_gather | solution.py:75
  7.9 40.9 %all-gather.8.cloned.1.call-start = ((), (), s32[]{:S(2)}) async-start(), calls=%async_computation.5 | async-start | bytes 1474560 | tf_op jit(solution)/shard_map/all_gather | solution.py:76
  8.7 27.8 %copy-start.12 = (bf16[256,1,384]{2,0,1:T(8,128)(2,1)S(1)}, bf16[256,1,384]{2,0,1:T(8,128)(2,1)}, u32[]{:S(2)}) copy-start(bf16[256,1,384]{2,0,1:T(8,128)(2,1)} %param.13) | copy-start | bytes 589828
  8.7 27.9 %copy-start.13 = (bf16[256,1,384]{2,0,1:T(8,128)(2,1)S(1)}, bf16[256,1,384]{2,0,1:T(8,128)(2,1)}, u32[]{:S(2)}) copy-start(bf16[256,1,384]{2,0,1:T(8,128)(2,1)} %param.14) | copy-start | bytes 589828
  8.7 28.1 %copy-start.14 = (s32[256,1]{0,1:T(1,128)S(1)}, s32[256,1]{0,1:T(1,128)}, u32[]{:S(2)}) copy-start(s32[256,1]{0,1:T(1,128)} %param.15) | copy-start | bytes 3076
  8.7 95.0 %all-gather.6.cloned.1.call-start = ((), (), s32[]{:S(2)}) async-start(), calls=%async_computation.4 | async-start | bytes 2654208 | tf_op jit(solution)/shard_map/all_gather | solution.py:106
  36.4 181.1 %reduce-scatter.6.cloned.1.call-start = ((), (), s32[]{:S(2)}) async-start(), calls=%async_computation.6 | async-start | bytes 2654208 | tf_op jit(solution)/shard_map/reduce_scatter | solution.py:152
  38.5 12.4 %copy-start.8 = (bf16[192,1,3,128]{3,2,0,1:T(4,128)(2,1)S(1)}, bf16[192,1,3,128]{3,2,0,1:T(4,128)(2,1)}, u32[]{:S(2)}) copy-start(bf16[192,1,3,128]{3,2,0,1:T(4,128)(2,1)} %reshape_squeeze.3) | copy-start | bytes 442372
  110.0 1.8 copy-start.2
  119.5 4.3 copy-start.3
  119.5 4.3 copy-start.4
  128.1 1.7 copy-start.5
  129.9 1.4 copy-start.6
  134.1 1.7 copy-start.5
  135.9 1.4 copy-start.6
  149.8 141.9 %all-reduce.3.cloned.1.call-start = ((), (), s32[]{:S(2)}) async-start(), calls=%async_computation.9 | async-start | bytes 786432
  155.0 62.5 %copy-start.7 = (bf16[192,1,3072]{2,0,1:T(8,128)(2,1)S(1)}, bf16[192,1,3072]{2,0,1:T(8,128)(2,1)}, u32[]{:S(2)}) copy-start(bf16[192,1,3072]{2,0,1:T(8,128)(2,1)} %all-gather.4.cloned.1.call-done) | copy-start | bytes 3538948
  155.0 303.0 %reduce-scatter.10.cloned.1.call-start = ((), (), s32[]{:S(2)}) async-start(), calls=%async_computation.8 | async-start | bytes 10616832
  243.7 0.9 copy-start.9
  243.7 1.0 copy-start.11
  243.7 7.6 %copy-start.15 = (u32[32]{0:T(128)S(1)}, u32[32]{0:T(128)}, u32[]{:S(2)}) copy-start(u32[32]{0:T(128)} %constant.13) | copy-start | bytes 388
  243.8 242.5 %reduce-scatter.8.cloned.1.call-start = ((), (), s32[]{:S(2)}) async-start(), calls=%async_computation.7 | async-start | bytes 1474560 | tf_op jit(solution)/shard_map/reduce_scatter | solution.py:162
  461.1 25.1 %copy-start.1 = (bf16[3072,384]{1,0:T(8,128)(2,1)S(1)}, bf16[3072,384]{1,0:T(8,128)(2,1)}, u32[]{:S(2)}) copy-start(bf16[3072,384]{1,0:T(8,128)(2,1)} %param.12) | copy-start | bytes 7077892
  (1 other events, 0.8 us)
Sparse Core Ops, SparseCore 0:
  9.6 20.1 all-gather.3
  31.3 17.4 all-gather.7
  51.6 52.0 all-gather.5
  149.9 67.4 reduce-scatter.5
  221.2 70.3 all-reduce.2
  295.5 162.4 reduce-scatter.9
  461.4 24.8 reduce-scatter.7
where the time goes:
time: 494 us; the launch traced here: 493 us
  waiting for transfers between devices  368 us (74%)
  local copies, waits for them, and re-layouts  65.3 us (13%)
  matrix products  31.2 us (6%)
  between operations  15.1 us (3%)
  other arithmetic  13.2 us (3%)
    unnamed x9, waiting for transfers between devices  205 us
    reduce_scatter x1, waiting for transfers between devices, per_device(): lax.psum_scatter(key_terms.astype(jnp.bfloat16), 'blk', scatter_dimension...  60.1 us
    all_gather x1, waiting for transfers between devices, per_device(): kv_piece = lax.all_gather(kv_local, 'blk', axis=0, tiled=True)  52.4 us
    unnamed x35, local copies, waits for them, and re-layouts  22.4 us
    all_gather x1, waiting for transfers between devices, per_device(): lax.all_gather(inputs, 'head', axis=2, tiled=True)  21 us
    reduce_scatter x1, waiting for transfers between devices, per_device(): lax.psum_scatter(input_terms.astype(jnp.bfloat16), 'head', scatter_dimens...  18.5 us
    convert_element_type x2, local copies, waits for them, and re-layouts, per_device(): key_terms.astype(jnp.bfloat16)  12.4 us
    all_gather x1, waiting for transfers between devices, per_device(): lax.all_gather(out_grad, 'head', axis=2, tiled=True)  10.3 us
  transfers between devices with their start and end apart: 7, of which 7 were waited for; matrix products, arithmetic and copies ran while one was open for 13% of the time, Pallas kernels for 0%

commit v1 on v0

--- a/solution.py
+++ b/solution.py
@@ -1,6 +1,10 @@
+import functools
+
 import jax
 import jax.numpy as jnp
 from jax import lax
+from jax.experimental import pallas as pl
+from jax.experimental.pallas import tpu as pltpu
 from jax.sharding import PartitionSpec as P
 
 HD = 128
@@ -70,7 +74,7 @@
     )
 
 
-def per_device(inputs, out_grad, qkv_weight, out_weight, text_keys, text_values, text_mask):
+def plain_device(inputs, out_grad, qkv_weight, out_weight, text_keys, text_values, text_mask):
     full_in, full_grad = (
         lax.all_gather(inputs, "head", axis=2, tiled=True),
         lax.all_gather(out_grad, "head", axis=2, tiled=True),
@@ -181,6 +185,467 @@
     )
 
 
+MESH = pl.DeviceIdType.MESH
+LOG2E = 1.4426950408889634
+VMEM_BYTES = 60 * 1024 * 1024
+
+
+def dot(a, b, contract=((1,), (0,))):
+    return lax.dot_general(a, b, (contract, ((), ())), preferred_element_type=jnp.float32)
+
+
+def fused_kernel(
+    n,
+    tile,
+    x_hbm,
+    g_hbm,
+    wqkv_hbm,
+    wout_hbm,
+    tk_ref,
+    tv_ref,
+    mask_ref,
+    dx_ref,
+    dwqkv_ref,
+    dwout_ref,
+    dtk_ref,
+    dtv_ref,
+    full,
+    weights,
+    proj,
+    ring,
+    cols_in,
+    cols_t,
+    keys,
+    values,
+    keys_t,
+    values_t,
+    grad_k,
+    grad_v,
+    gp,
+    pair_out,
+    pair_in,
+    cross_out,
+    cross_in,
+    load_sem,
+    head_send,
+    head_recv,
+    ring_send,
+    ring_recv,
+    own_sem,
+    swap_send,
+    swap_recv,
+    col_send,
+    col_recv,
+    red_send,
+    red_recv,
+):
+    rows, depth = full.shape[1], full.shape[2]
+    feats = x_hbm.shape[1]
+    heads = ring.shape[0]
+    text = tk_ref.shape[0]
+    total_rows = ring.shape[2]
+    width = cols_in.shape[3]
+    quarter = rows // 4
+    tiles = total_rows // tile
+    half = n // 2
+    scale = HD ** (-0.5)
+
+    hd = lax.axis_index("head")
+    me = lax.axis_index("blk")
+    sib = hd + 1 - 2 * (hd % 2)
+    far = (hd + 2) % 4
+    diag = (sib + 2) % 4
+    odd = me % 2
+    pos = (1 - odd) * (me // 2) + odd * (n - 1 - me // 2)
+
+    def blk_at(p):
+        p = p % n
+        hi = p // half
+        return (1 - hi) * (2 * p) + hi * (2 * (n - 1 - p) + 1)
+
+    right, left = blk_at(pos + 1), blk_at(pos + n - 1)
+
+    def feat(j):
+        return pl.ds(pl.multiple_of(j * feats, 128), feats)
+
+    def block(j):
+        return pl.ds(pl.multiple_of(j * rows, 16), rows)
+
+    w_loads = [
+        pltpu.make_async_copy(wqkv_hbm, weights.at[pl.ds(0, 3)], load_sem.at[2]),
+        pltpu.make_async_copy(wout_hbm, weights.at[3], load_sem.at[3]),
+    ]
+    own_loads = [
+        pltpu.make_async_copy(src, full.at[a, :, feat(hd)], load_sem.at[a])
+        for a, src in enumerate((x_hbm, g_hbm))
+    ]
+    for c in own_loads + w_loads:
+        c.start()
+
+    barrier = pltpu.get_barrier_semaphore()
+    for r in range(1, n):
+        pl.semaphore_signal(
+            barrier, inc=1, device_id={"blk": (me + r) % n}, device_id_type=MESH
+        )
+    for other in (sib, far):
+        pl.semaphore_signal(barrier, inc=1, device_id={"head": other}, device_id_type=MESH)
+    pl.semaphore_wait(barrier, n + 1)
+
+    def head_copy(a, kind):
+        j = far if kind == 2 else hd
+        ref = full.at[a, :, feat(j)]
+        return pltpu.make_async_remote_copy(
+            src_ref=ref,
+            dst_ref=ref,
+            send_sem=head_send.at[a, kind],
+            recv_sem=head_recv.at[a, kind],
+            device_id={"head": far if kind == 0 else sib},
+            device_id_type=MESH,
+        )
+
+    for a in range(2):
+        own_loads[a].wait()
+        head_copy(a, 0).start()
+        head_copy(a, 1).start()
+
+    def project(a, j, first=False):
+        part = full[a, :, feat(j)]
+        for c in (0, 1, 2) if a == 0 else (3,):
+            term = dot(part, weights[c, feat(j), :])
+            proj[c] = term if first else proj[c] + term
+
+    for c in w_loads:
+        c.wait()
+    for a in range(2):
+        project(a, hd, True)
+    for a in range(2):
+        head_copy(a, 1).wait_recv()
+        project(a, sib)
+    for a in range(2):
+        head_copy(a, 0).wait_recv()
+        head_copy(a, 2).start()
+        project(a, far)
+    for a in range(2):
+        head_copy(a, 2).wait_recv()
+        project(a, diag)
+    for h in range(heads):
+        for c in range(4):
+            ring[h, c, block(me), :] = proj[c, :, h * HD : (h + 1) * HD].astype(jnp.bfloat16)
+
+    def ring_copy(h, s, way):
+        p = pos - (s - 1) + n if way == 0 else pos + s - 1
+        j = blk_at(p)
+        if s < half:
+            ref = ring.at[h, :, block(j), :]
+        else:
+            ref = ring.at[h, pl.ds(2 * way, 2), block(j), :]
+        return pltpu.make_async_remote_copy(
+            src_ref=ref,
+            dst_ref=ref,
+            send_sem=ring_send.at[h, s - 1, way],
+            recv_sem=ring_recv.at[h, s - 1, way],
+            device_id={"blk": right if way == 0 else left},
+            device_id_type=MESH,
+        )
+
+    def hop(h, s):
+        for way in range(2):
+            if s > 1:
+                ring_copy(h, s - 1, way).wait_recv()
+            ring_copy(h, s, way).start()
+
+    def finish(h):
+        for way in range(2):
+            ring_copy(h, half, way).wait_recv()
+            for s in range(1, half + 1):
+                ring_copy(h, s, way).wait_send()
+
+    mine = pl.ds(pl.multiple_of(hd * quarter, 16), quarter)
+
+    def wide(j):
+        return pl.ds(pl.multiple_of(j * width, 128), width)
+
+    def swap_copy(r):
+        to = (me + r) % n
+        return pltpu.make_async_remote_copy(
+            src_ref=full.at[:, mine, wide(to)],
+            dst_ref=cols_in.at[:, me, mine, :],
+            send_sem=swap_send.at[r],
+            recv_sem=swap_recv.at[r],
+            device_id={"blk": to},
+            device_id_type=MESH,
+        )
+
+    own_cols = pltpu.make_async_copy(
+        full.at[:, mine, wide(me)], cols_in.at[:, me, mine, :], own_sem.at[0]
+    )
+
+    def swap_start():
+        own_cols.start()
+        for r in range(1, n):
+            swap_copy(r).start()
+
+    def col_copy(kind):
+        j = far if kind == 2 else hd
+        ref = cols_in.at[:, :, pl.ds(pl.multiple_of(j * quarter, 16), quarter), :]
+        return pltpu.make_async_remote_copy(
+            src_ref=ref,
+            dst_ref=ref,
+            send_sem=col_send.at[kind],
+            recv_sem=col_recv.at[kind],
+            device_id={"head": far if kind == 0 else sib},
+            device_id_type=MESH,
+        )
+
+    def cols_start():
+        own_cols.wait()
+        for r in range(1, n):
+            swap_copy(r).wait_recv()
+        col_copy(0).start()
+        col_copy(1).start()
+
+    def cols_forward():
+        col_copy(0).wait_recv()
+        col_copy(2).start()
+
+    def attend(h, events):
+        lanes = pl.ds(h * HD, HD)
+        keys[pl.ds(0, text), :] = tk_ref[:, lanes]
+        keys[pl.ds(text, total_rows), :] = ring[h, 1]
+        values[pl.ds(0, text), :] = tv_ref[:, lanes]
+        values[pl.ds(text, total_rows), :] = ring[h, 2]
+        keys_t[...] = keys[...].T
+        values_t[...] = values[...].T
+        grad_k[...] = jnp.zeros_like(grad_k)
+        grad_v[...] = jnp.zeros_like(grad_v)
+
+        @pl.loop(0, tiles)
+        def _(i):
+            for at, run in events:
+                pl.when(i == at)(run)
+            here = pl.ds(pl.multiple_of(i * tile, tile), tile)
+            q = ring[h, 0, here, :]
+            go = ring[h, 3, here, :]
+            go_t = go.T
+            logits = dot(keys[...], q.T)
+            logits = jnp.concatenate(
+                [jnp.where(mask_ref[...] > 0.0, logits[:text], masked_fill / scale), logits[text:]],
+                axis=0,
+            )
+            top = jnp.max(logits, axis=0, keepdims=True)
+            p = jnp.exp2((logits - top) * (scale * LOG2E))
+            inv = 1.0 / jnp.sum(p, axis=0, keepdims=True)
+            pb = p.astype(jnp.bfloat16)
+            out_t = (dot(values_t[...], pb) * inv).astype(jnp.bfloat16)
+            go_f = go_t.astype(jnp.float32)
+            row_dot = jnp.sum(go_f * out_t.astype(jnp.float32), axis=0, keepdims=True)
+            gp_t = dot(values[...], go_t)
+            ds = (p * ((gp_t - row_dot) * (inv * scale))).astype(jnp.bfloat16)
+            dq_t = dot(keys_t[...], ds)
+            grad_k[...] += dot(ds, q)
+            grad_v[...] += dot(pb, (go_f * inv).astype(jnp.bfloat16).T)
+            ring[h, 0, here, :] = dq_t.astype(jnp.bfloat16).T
+            ring[h, 3, here, :] = out_t.T
+
+        ring[h, 1] = grad_k[pl.ds(text, total_rows), :].astype(jnp.bfloat16)
+        ring[h, 2] = grad_v[pl.ds(text, total_rows), :].astype(jnp.bfloat16)
+        part = text // n
+        own_text = pl.ds(pl.multiple_of(me * part, 8), part)
+        dtk_ref[:, lanes] = grad_k[own_text, :]
+        dtv_ref[:, lanes] = grad_v[own_text, :]
+
+    order = []
+    for h in range(heads):
+        order += [(h, s) for s in range(2 if h else 1, half)]
+        if h + 1 < heads:
+            order.append((h + 1, 1))
+        order.append((h, half))
+    for h, s in order[: half + 1]:
+        hop(h, s)
+    rest = order[half + 1 :]
+    for h in range(heads):
+        finish(h)
+        if h + 1 < heads:
+            todo = [functools.partial(hop, *e) for e in rest[:half]] if h + 2 < heads else [
+                functools.partial(hop, *e) for e in rest
+            ]
+            rest = rest[half:]
+            if h + 2 == heads:
+                todo.append(swap_start)
+        else:
+            todo = [cols_start, cols_forward]
+        if h + 1 < heads:
+            events = [(min(tiles - 1, e * tiles // len(todo)), run) for e, run in enumerate(todo)]
+        else:
+            events = [(tiles // 2, todo[0]), (tiles - 1, todo[1])]
+        attend(h, events)
+
+    for h in range(heads):
+        for c in range(3):
+            gp[c, :, pl.ds(h * HD, HD)] = ring[h, c, block(me), :]
+
+    def input_term(j):
+        return sum(dot(gp[c], weights[c, feat(j), :], ((1,), (1,))) for c in range(3))
+
+    def pair_copy(k):
+        return pltpu.make_async_remote_copy(
+            src_ref=pair_out.at[k],
+            dst_ref=pair_in.at[k],
+            send_sem=red_send.at[k],
+            recv_sem=red_recv.at[k],
+            device_id={"head": sib},
+            device_id_type=MESH,
+        )
+
+    cross_copy = pltpu.make_async_remote_copy(
+        src_ref=cross_out,
+        dst_ref=cross_in,
+        send_sem=red_send.at[2],
+        recv_sem=red_recv.at[2],
+        device_id={"head": far},
+        device_id_type=MESH,
+    )
+    pair_out[1] = input_term(diag).astype(jnp.bfloat16)
+    pair_copy(1).start()
+    pair_out[0] = input_term(sib).astype(jnp.bfloat16)
+    pair_copy(0).start()
+    far_term = input_term(far)
+    pair_copy(1).wait_recv()
+    cross_out[...] = (far_term + pair_in[1].astype(jnp.float32)).astype(jnp.bfloat16)
+    cross_copy.start()
+    own_term = input_term(hd)
+    pair_copy(0).wait_recv()
+    own_term = own_term + pair_in[0].astype(jnp.float32)
+
+    col_copy(1).wait_recv()
+    col_copy(2).wait_recv()
+    for a in range(2):
+        cols_t[a] = cols_in[a].reshape(total_rows, width).T
+    for h in range(heads):
+        lanes = pl.ds(h * HD, HD)
+        three = jnp.concatenate([ring[h, 0], ring[h, 1], ring[h, 2]], axis=1)
+        term = dot(cols_t[0], three)
+        for c in range(3):
+            dwqkv_ref[c, :, lanes] = term[:, c * HD : (c + 1) * HD]
+        dwout_ref[:, lanes] = dot(cols_t[1], ring[h, 3])
+
+    cross_copy.wait_recv()
+    dx_ref[...] = (own_term + cross_in[...].astype(jnp.float32)).astype(jnp.bfloat16)
+
+    for a in range(2):
+        for kind in range(3):
+            head_copy(a, kind).wait_send()
+    for r in range(1, n):
+        swap_copy(r).wait_send()
+    for kind in range(3):
+        col_copy(kind).wait_send()
+    pair_copy(0).wait_send()
+    pair_copy(1).wait_send()
+    cross_copy.wait_send()
+
+
+def fused_device(inputs, out_grad, qkv_weight, out_weight, text_keys, text_values, text_mask):
+    n = lax.axis_size("blk")
+    rows, _, feats = inputs.shape
+    depth, _, local = qkv_weight.shape
+    text = text_keys.shape[0]
+    heads = local // HD
+    total_rows = rows * n
+    length = text + total_rows
+    width = depth // n
+    tile = 256
+    bf, f32 = jnp.bfloat16, jnp.float32
+    mask = jnp.broadcast_to((text_mask == 1).astype(f32), (text, tile))
+    vmem = pl.BlockSpec(memory_space=pltpu.VMEM)
+    hbm = pl.BlockSpec(memory_space=pl.ANY)
+    dma = pltpu.SemaphoreType.DMA
+    outs = pl.pallas_call(
+        functools.partial(fused_kernel, n, tile),
+        out_shape=(
+            jax.ShapeDtypeStruct((rows, feats), bf),
+            jax.ShapeDtypeStruct((3, width, local), f32),
+            jax.ShapeDtypeStruct((width, local), f32),
+            jax.ShapeDtypeStruct((text // n, local), f32),
+            jax.ShapeDtypeStruct((text // n, local), f32),
+        ),
+        in_specs=[hbm] * 4 + [vmem] * 3,
+        out_specs=[vmem] * 5,
+        scratch_shapes=[
+            pltpu.VMEM((2, rows, depth), bf),
+            pltpu.VMEM((4, depth, local), bf),
+            pltpu.VMEM((4, rows, local), f32),
+            pltpu.VMEM((heads, 4, total_rows, HD), bf),
+            pltpu.VMEM((2, n, rows, width), bf),
+            pltpu.VMEM((2, width, total_rows), bf),
+            pltpu.VMEM((length, HD), bf),
+            pltpu.VMEM((length, HD), bf),
+            pltpu.VMEM((HD, length), bf),
+            pltpu.VMEM((HD, length), bf),
+            pltpu.VMEM((length, HD), f32),
+            pltpu.VMEM((length, HD), f32),
+            pltpu.VMEM((3, rows, local), bf),
+            pltpu.VMEM((2, rows, feats), bf),
+            pltpu.VMEM((2, rows, feats), bf),
+            pltpu.VMEM((rows, feats), bf),
+            pltpu.VMEM((rows, feats), bf),
+            dma((4,)),
+            dma((2, 3)),
+            dma((2, 3)),
+            dma((heads, n // 2, 2)),
+            dma((heads, n // 2, 2)),
+            dma((1,)),
+            dma((n,)),
+            dma((n,)),
+            dma((3,)),
+            dma((3,)),
+            dma((3,)),
+            dma((3,)),
+        ],
+        compiler_params=pltpu.CompilerParams(
+            collective_id=0, has_side_effects=True, vmem_limit_bytes=VMEM_BYTES
+        ),
+        cost_estimate=pl.CostEstimate(
+            flops=2 * heads * 6 * total_rows * length * HD + 16 * rows * depth * local,
+            bytes_accessed=16 * depth * local,
+            transcendentals=heads * total_rows * length,
+        ),
+    )(
+        inputs.reshape(rows, feats),
+        out_grad.reshape(rows, feats),
+        jnp.transpose(qkv_weight, (1, 0, 2)),
+        out_weight,
+        text_keys.reshape(text, local),
+        text_values.reshape(text, local),
+        mask,
+    )
+    dx, dwqkv, dwout, dtk, dtv = outs
+    return (
+        dx.reshape(rows, 1, feats),
+        jnp.transpose(dwqkv, (1, 0, 2)),
+        dwout,
+        dtk.reshape(text // n, 1, local),
+        dtv.reshape(text // n, 1, local),
+    )
+
+
+def per_device(inputs, out_grad, qkv_weight, out_weight, text_keys, text_values, text_mask):
+    n = lax.axis_size("blk")
+    rows, seqs, _ = inputs.shape
+    depth = qkv_weight.shape[0]
+    fits = (
+        seqs == 1
+        and lax.axis_size("head") == 4
+        and n % 2 == 0
+        and rows % 64 == 0
+        and (rows * n) % 256 == 0
+        and rows * n <= 2048
+        and depth % (128 * n) == 0
+        and text_keys.shape[0] % (8 * n) == 0
+    )
+    chosen = fused_device if fits else plain_device
+    return chosen(inputs, out_grad, qkv_weight, out_weight, text_keys, text_values, text_mask)
+
+
 def solution(mesh):
     return jax.shard_map(
         per_device,

time: 494 us -> 131 us (0.27)
  waiting for transfers between devices: 368 us -> 0 us
  Pallas kernels: 0 us -> 120 us
  local copies, waits for them, and re-layouts: 65.3 us -> 9.11 us
  matrix products: 31.2 us -> 0 us
  between operations: 15.1 us -> 0.65 us
  other arithmetic: 13.2 us -> 0.68 us
    unnamed x9 -> x0, waiting for transfers between devices: 205 us -> none
    pallas_call x0 -> x1, Pallas kernels: none -> 120 us  [fused_device(): pl.pallas_call(functools.partial(fused_kernel, n, tile), out_shape=(jax.S...]
    all_gather x3 -> x0, waiting for transfers between devices: 83.7 us -> none  [the longest x1 52.4 us: per_device(): kv_piece = lax.all_gather(kv_local, 'blk', axis=0, tiled=True)]
    reduce_scatter x2 -> x0, waiting for transfers between devices: 78.6 us -> none  [the longest x1 60.1 us: per_device(): lax.psum_scatter(key_terms.astype(jnp.bfloat16), 'blk', scatter_dimension...]
    dot_general x23 -> x0, matrix products: 31.2 us -> none  [the longest x1 6.54 us: per_device(): jnp.einsum('vsch,dch->vsd', grad_projected, qkv_weight, preferred_element...]
    unnamed x35 -> x7, local copies, waits for them, and re-layouts: 22.4 us -> 8.31 us
    convert_element_type x4 -> x0, local copies, waits for them, and re-layouts: 13.4 us -> none  [the longest x2 12.4 us: per_device(): key_terms.astype(jnp.bfloat16)]
    while x10 -> x0, local copies, waits for them, and re-layouts: 8.17 us -> none
  transfers between devices with their start and end apart: 7 -> 0, of which waited for: 7 -> 0; matrix products, arithmetic and copies ran while one was open for 13% -> 0% of each run, Pallas kernels for 0% -> 0%
where the time goes in v1:
time: 131 us
  Pallas kernels  120 us (92%)
  local copies, waits for them, and re-layouts  9.11 us (7%)
    pallas_call x1, Pallas kernels, fused_device(): pl.pallas_call(functools.partial(fused_kernel, n, tile), out_shape=(jax.S...  120 us
    unnamed x7, local copies, waits for them, and re-layouts  8.31 us

profile of v1, /device:TPU:0, one launch (start us, length us, event | category | flops | bytes accessed | tf_op | source)
XLA Modules:
  0.0 130.6 jit_solution(3101296706917001151)
XLA Ops:
  0.6 0.7 compare_convert_fusion
  1.3 0.8 broadcast_in_dim.12.mask_ref
  2.1 120.1 %shard_map.110 = (bf16[192,768]{1,0:T(8,128)(2,1)}, f32[3,384,384]{2,1,0:T(8,128)}, f32[384,384]{1,0:T(8,128)}, f32[32,384]{1,0:T(8,128)}, f32[32,384]{1,0:T(8,128)}) custom-call(bf16[192,768]{1,0:T(8,128)(2,1)} %bitcast.16, bf16[192,768]{1,0:T(8,128)(2,1)} %bitcast.17, bf16[3,3072,384]{2,1,0:T(8,128)(2,1)} %bitcast.15, bf16[3072,384]{1,0:T(8,128)(2,1)} %wout_hbm.1, ...), custom_call_target="tpu_custom_call" | custom-call | flops 16307453952 | bytes 18874368 | tf_op jit(solution)/shard_map/pallas_call | solution.py:562
  122.3 0.0 copy-start
  122.3 1.5 %copy.12 = f32[32,1,384]{2,1,0:T(1,128)} copy(f32[32,1,384]{2,0,1:T(8,128)} %bitcast.13) | data formatting | bytes 98304
  123.8 1.5 %copy.13 = f32[32,1,384]{2,1,0:T(1,128)} copy(f32[32,1,384]{2,0,1:T(8,128)} %bitcast.12) | data formatting | bytes 98304
  125.3 1.7 %copy.17 = bf16[192,1,768]{2,0,1:T(8,128)(2,1)} copy(bf16[192,1,768]{2,0,1:T(8,128)(2,1)} %bitcast.11) | data formatting | bytes 589824
  127.0 2.8 %copy.18 = f32[384,3,384]{2,0,1:T(8,128)} copy(f32[384,3,384]{2,0,1:T(8,128)} %bitcast.10) | data formatting | bytes 3538944
  129.8 0.0 copy-done
  129.8 0.8 copy.19
Async XLA Ops:
  122.3 7.5 %copy-start = (f32[384,384]{1,0:T(8,128)S(1)}, f32[384,384]{1,0:T(8,128)}, u32[]{:S(2)}) copy-start(f32[384,384]{1,0:T(8,128)} %get-tuple-element.27) | copy-start | bytes 1769476

commit v2 on v1

--- a/solution.py
+++ b/solution.py
@@ -303,10 +303,11 @@
             device_id_type=MESH,
         )
 
-    for a in range(2):
-        own_loads[a].wait()
-        head_copy(a, 0).start()
-        head_copy(a, 1).start()
+    own_loads[0].wait()
+    head_copy(0, 0).start()
+    head_copy(0, 1).start()
+    own_loads[1].wait()
+    head_copy(1, 1).start()
 
     def project(a, j, first=False):
         part = full[a, :, feat(j)]
@@ -314,51 +315,70 @@
             term = dot(part, weights[c, feat(j), :])
             proj[c] = term if first else proj[c] + term
 
-    for c in w_loads:
-        c.wait()
-    for a in range(2):
-        project(a, hd, True)
-    for a in range(2):
-        head_copy(a, 1).wait_recv()
-        project(a, sib)
-    for a in range(2):
-        head_copy(a, 0).wait_recv()
-        head_copy(a, 2).start()
-        project(a, far)
-    for a in range(2):
-        head_copy(a, 2).wait_recv()
-        project(a, diag)
-    for h in range(heads):
-        for c in range(4):
+    def place(c):
+        for h in range(heads):
             ring[h, c, block(me), :] = proj[c, :, h * HD : (h + 1) * HD].astype(jnp.bfloat16)
 
-    def ring_copy(h, s, way):
+    def ring_copy(h, g, s, way):
+        first, last = (0, 4) if h else ((0, 3), (3, 4))[g]
+        if s == half:
+            first, last = max(first, 2 * way), min(last, 2 * way + 2)
+        if first >= last:
+            return None
         p = pos - (s - 1) + n if way == 0 else pos + s - 1
-        j = blk_at(p)
-        if s < half:
-            ref = ring.at[h, :, block(j), :]
-        else:
-            ref = ring.at[h, pl.ds(2 * way, 2), block(j), :]
+        ref = ring.at[h, pl.ds(first, last - first), block(blk_at(p)), :]
         return pltpu.make_async_remote_copy(
             src_ref=ref,
             dst_ref=ref,
-            send_sem=ring_send.at[h, s - 1, way],
-            recv_sem=ring_recv.at[h, s - 1, way],
+            send_sem=ring_send.at[h, g, s - 1, way],
+            recv_sem=ring_recv.at[h, g, s - 1, way],
             device_id={"blk": right if way == 0 else left},
             device_id_type=MESH,
         )
 
-    def hop(h, s):
+    def hop(h, g, s):
         for way in range(2):
             if s > 1:
-                ring_copy(h, s - 1, way).wait_recv()
-            ring_copy(h, s, way).start()
+                ring_copy(h, g, s - 1, way).wait_recv()
+            copy = ring_copy(h, g, s, way)
+            if copy is not None:
+                copy.start()
 
     def finish(h):
-        for way in range(2):
-            ring_copy(h, half, way).wait_recv()
-            for s in range(1, half + 1):
-                ring_copy(h, s, way).wait_send()
+        for g in range(1 if h else 2):
+            for way in range(2):
+                for s in range(1, half + 1):
+                    copy = ring_copy(h, g, s, way)
+                    if copy is not None:
+                        if s == half:
+                            copy.wait_recv()
+                        copy.wait_send()
+
+    for c in w_loads:
+        c.wait()
+    project(0, hd, True)
+    head_copy(0, 1).wait_recv()
+    project(0, sib)
+    head_copy(0, 0).wait_recv()
+    head_copy(0, 2).start()
+    head_copy(1, 0).start()
+    project(0, far)
+    head_copy(0, 2).wait_recv()
+    project(0, diag)
+    for c in range(3):
+        place(c)
+    hop(0, 0, 1)
+    project(1, hd, True)
+    head_copy(1, 1).wait_recv()
+    project(1, sib)
+    hop(0, 0, 2)
+    head_copy(1, 0).wait_recv()
+    head_copy(1, 2).start()
+    project(1, far)
+    head_copy(1, 2).wait_recv()
+    project(1, diag)
+    place(3)
+    hop(0, 1, 1)
 
     mine = pl.ds(pl.multiple_of(hd * quarter, 16), quarter)
 
@@ -428,6 +448,7 @@
             go = ring[h, 3, here, :]
             go_t = go.T
             logits = dot(keys[...], q.T)
+            gp_t = dot(values[...], go_t)
             logits = jnp.concatenate(
                 [jnp.where(mask_ref[...] > 0.0, logits[:text], masked_fill / scale), logits[text:]],
                 axis=0,
@@ -438,12 +459,11 @@
             pb = p.astype(jnp.bfloat16)
             out_t = (dot(values_t[...], pb) * inv).astype(jnp.bfloat16)
             go_f = go_t.astype(jnp.float32)
+            grad_v[...] += dot(pb, (go_f * inv).astype(jnp.bfloat16).T)
             row_dot = jnp.sum(go_f * out_t.astype(jnp.float32), axis=0, keepdims=True)
-            gp_t = dot(values[...], go_t)
             ds = (p * ((gp_t - row_dot) * (inv * scale))).astype(jnp.bfloat16)
             dq_t = dot(keys_t[...], ds)
             grad_k[...] += dot(ds, q)
-            grad_v[...] += dot(pb, (go_f * inv).astype(jnp.bfloat16).T)
             ring[h, 0, here, :] = dq_t.astype(jnp.bfloat16).T
             ring[h, 3, here, :] = out_t.T
 
@@ -454,31 +474,26 @@
         dtk_ref[:, lanes] = grad_k[own_text, :]
         dtv_ref[:, lanes] = grad_v[own_text, :]
 
-    order = []
-    for h in range(heads):
-        order += [(h, s) for s in range(2 if h else 1, half)]
-        if h + 1 < heads:
-            order.append((h + 1, 1))
-        order.append((h, half))
-    for h, s in order[: half + 1]:
-        hop(h, s)
-    rest = order[half + 1 :]
+    for s in range(2, half):
+        hop(0, 1, s)
+        if s + 1 < half:
+            hop(0, 0, s + 1)
+    hop(1, 0, 1)
+    hop(0, 0, half)
+    hop(0, 1, half)
     for h in range(heads):
         finish(h)
+        todo = []
         if h + 1 < heads:
-            todo = [functools.partial(hop, *e) for e in rest[:half]] if h + 2 < heads else [
-                functools.partial(hop, *e) for e in rest
-            ]
-            rest = rest[half:]
-            if h + 2 == heads:
-                todo.append(swap_start)
-        else:
-            todo = [cols_start, cols_forward]
-        if h + 1 < heads:
-            events = [(min(tiles - 1, e * tiles // len(todo)), run) for e, run in enumerate(todo)]
-        else:
-            events = [(tiles // 2, todo[0]), (tiles - 1, todo[1])]
-        attend(h, events)
+            todo = [functools.partial(hop, h + 1, 0, s) for s in range(2, half + 1)]
+        if h + 2 < heads:
+            todo.insert(half - 2, functools.partial(hop, h + 2, 0, 1))
+        if h == 0:
+            todo.insert(0, swap_start)
+        if h == 1:
+            todo.insert(1, cols_start)
+            todo.append(cols_forward)
+        attend(h, [(e * tiles // len(todo), run) for e, run in enumerate(todo)])
 
     for h in range(heads):
         for c in range(3):
@@ -526,8 +541,8 @@
         three = jnp.concatenate([ring[h, 0], ring[h, 1], ring[h, 2]], axis=1)
         term = dot(cols_t[0], three)
         for c in range(3):
-            dwqkv_ref[c, :, lanes] = term[:, c * HD : (c + 1) * HD]
-        dwout_ref[:, lanes] = dot(cols_t[1], ring[h, 3])
+            dwqkv_ref[c, :, lanes] = term[:, c * HD : (c + 1) * HD].astype(jnp.bfloat16)
+        dwout_ref[:, lanes] = dot(cols_t[1], ring[h, 3]).astype(jnp.bfloat16)
 
     cross_copy.wait_recv()
     dx_ref[...] = (own_term + cross_in[...].astype(jnp.float32)).astype(jnp.bfloat16)
@@ -563,8 +578,8 @@
         functools.partial(fused_kernel, n, tile),
         out_shape=(
             jax.ShapeDtypeStruct((rows, feats), bf),
-            jax.ShapeDtypeStruct((3, width, local), f32),
-            jax.ShapeDtypeStruct((width, local), f32),
+            jax.ShapeDtypeStruct((3, width, local), bf),
+            jax.ShapeDtypeStruct((width, local), bf),
             jax.ShapeDtypeStruct((text // n, local), f32),
             jax.ShapeDtypeStruct((text // n, local), f32),
         ),
@@ -591,8 +606,8 @@
             dma((4,)),
             dma((2, 3)),
             dma((2, 3)),
-            dma((heads, n // 2, 2)),
-            dma((heads, n // 2, 2)),
+            dma((heads, 2, n // 2, 2)),
+            dma((heads, 2, n // 2, 2)),
             dma((1,)),
             dma((n,)),
             dma((n,)),
@@ -621,8 +636,8 @@
     dx, dwqkv, dwout, dtk, dtv = outs
     return (
         dx.reshape(rows, 1, feats),
-        jnp.transpose(dwqkv, (1, 0, 2)),
-        dwout,
+        jnp.transpose(dwqkv, (1, 0, 2)).astype(f32),
+        dwout.astype(f32),
         dtk.reshape(text // n, 1, local),
         dtv.reshape(text // n, 1, local),
     )

time: 131 us -> 131 us (level)
  local copies, waits for them, and re-layouts: 9.11 us -> 2.88 us
  other arithmetic: 0.68 us -> 4.08 us
  Pallas kernels: 120 us -> 123 us
    unnamed x7 -> x11, local copies, waits for them, and re-layouts: 8.31 us -> 2.07 us
    convert_element_type x0 -> x2, other arithmetic: none -> 3.4 us  [the longest x1 2.54 us: fused_device(): jnp.transpose(dwqkv, (1, 0, 2)).astype(f32)]
    pallas_call x1, Pallas kernels: 120 us -> 123 us  [fused_device(): pl.pallas_call(functools.partial(fused_kernel, n, tile), out_shape=(jax.S...]
where the time goes in v2:
time: 131 us; the launch traced here: 130 us
  Pallas kernels  123 us (94%)
  other arithmetic  4.08 us (3%)
  local copies, waits for them, and re-layouts  2.88 us (2%)
    pallas_call x1, Pallas kernels, fused_device(): pl.pallas_call(functools.partial(fused_kernel, n, tile), out_shape=(jax.S...  123 us

profile of v2, /device:TPU:0, one launch (start us, length us, event | category | flops | bytes accessed | tf_op | source)
XLA Modules:
  0.0 130.4 jit_solution(1862675024323537293)
XLA Ops:
  0.6 0.7 compare_convert_fusion
  1.3 0.8 broadcast_in_dim.12.mask_ref
  2.1 122.8 %shard_map.110 = (bf16[192,768]{1,0:T(8,128)(2,1)}, bf16[3,384,384]{2,1,0:T(8,128)(2,1)}, bf16[384,384]{1,0:T(8,128)(2,1)}, f32[32,384]{1,0:T(8,128)}, f32[32,384]{1,0:T(8,128)}) custom-call(bf16[192,768]{1,0:T(8,128)(2,1)} %bitcast.16, bf16[192,768]{1,0:T(8,128)(2,1)} %bitcast.17, bf16[3,3072,384]{2,1,0:T(8,128)(2,1)} %bitcast.15, ...), custom_call_target="tpu_custom_call" | custom-call | flops 16307453952 | bytes 18874368 | tf_op jit(solution)/shard_map/pallas_call | solution.py:577
  124.9 0.0 copy-start
  124.9 0.0 copy-start.3
  124.9 0.0 copy-start.2
  125.0 0.0 copy-start.1
  125.0 2.5 %convert_bitcast_fusion = f32[384,3,384]{2,0,1:T(8,128)} fusion(bf16[3,384,384]{2,1,0:T(8,128)(2,1)} %get-tuple-element.11), kind=kLoop, calls=%fused_computation | loop fusion | flops 442368 | bytes 2654208 | tf_op jit(solution)/shard_map/convert_element_type | solution.py:639
  127.5 0.0 copy-done
  127.5 0.9 convert_element_type.12
  128.4 0.0 copy-done.3
  128.4 0.7 copy.12
  129.0 0.0 copy-done.2
  129.0 0.7 copy.13
  129.7 0.0 copy-done.1
  129.7 0.7 copy.15
Async XLA Ops:
  124.9 2.6 %copy-start = (bf16[384,384]{1,0:T(8,128)(2,1)S(1)}, bf16[384,384]{1,0:T(8,128)(2,1)}, u32[]{:S(2)}) copy-start(bf16[384,384]{1,0:T(8,128)(2,1)} %get-tuple-element.12) | copy-start | bytes 884740
  124.9 3.4 %copy-start.3 = (f32[32,384]{1,0:T(8,128)S(1)}, f32[32,384]{1,0:T(8,128)}, u32[]{:S(2)}) copy-start(f32[32,384]{1,0:T(8,128)} %get-tuple-element.13) | copy-start | bytes 147460
  124.9 4.1 %copy-start.2 = (f32[32,384]{1,0:T(8,128)S(1)}, f32[32,384]{1,0:T(8,128)}, u32[]{:S(2)}) copy-start(f32[32,384]{1,0:T(8,128)} %get-tuple-element.14) | copy-start | bytes 147460
  125.0 4.8 %copy-start.1 = (bf16[192,768]{1,0:T(8,128)(2,1)S(1)}, bf16[192,768]{1,0:T(8,128)(2,1)}, u32[]{:S(2)}) copy-start(bf16[192,768]{1,0:T(8,128)(2,1)} %get-tuple-element.10) | copy-start | bytes 884740

commit v3 on v2

--- a/solution.py
+++ b/solution.py
@@ -249,6 +249,8 @@
     tiles = total_rows // tile
     half = n // 2
     scale = HD ** (-0.5)
+    chunk = 512
+    chunks = [(0, text)] + [(text + k * chunk, chunk) for k in range(total_rows // chunk)]
 
     hd = lax.axis_index("head")
     me = lax.axis_index("blk")
@@ -446,27 +448,53 @@
             here = pl.ds(pl.multiple_of(i * tile, tile), tile)
             q = ring[h, 0, here, :]
             go = ring[h, 3, here, :]
+            q_t = q.T
             go_t = go.T
-            logits = dot(keys[...], q.T)
-            gp_t = dot(values[...], go_t)
-            logits = jnp.concatenate(
-                [jnp.where(mask_ref[...] > 0.0, logits[:text], masked_fill / scale), logits[text:]],
-                axis=0,
+            logits = []
+            top = None
+            for c, (first, size) in enumerate(chunks):
+                part = dot(keys[pl.ds(first, size), :], q_t)
+                if c == 0:
+                    part = jnp.where(mask_ref[...] > 0.0, part, masked_fill / scale)
+                high = jnp.max(part, axis=0, keepdims=True)
+                top = high if c == 0 else jnp.maximum(top, high)
+                logits.append(part)
+            top = top * (scale * LOG2E)
+            weights_b = []
+            total = out_t = 0.0
+            for (first, size), part in zip(chunks, logits):
+                p = jnp.exp2(part * (scale * LOG2E) - top)
+                total = total + jnp.sum(p, axis=0, keepdims=True)
+                pb = p.astype(jnp.bfloat16)
+                out_t = out_t + dot(values_t[:, pl.ds(first, size)], pb)
+                weights_b.append(pb)
+            inv = 1.0 / total
+            out_t = (out_t * inv).astype(jnp.bfloat16)
+            go_s = (go_t.astype(jnp.float32) * inv).astype(jnp.bfloat16)
+            row_dot = jnp.sum(
+                go_s.astype(jnp.float32) * out_t.astype(jnp.float32), axis=0, keepdims=True
             )
-            top = jnp.max(logits, axis=0, keepdims=True)
-            p = jnp.exp2((logits - top) * (scale * LOG2E))
-            inv = 1.0 / jnp.sum(p, axis=0, keepdims=True)
-            pb = p.astype(jnp.bfloat16)
-            out_t = (dot(values_t[...], pb) * inv).astype(jnp.bfloat16)
-            go_f = go_t.astype(jnp.float32)
-            grad_v[...] += dot(pb, (go_f * inv).astype(jnp.bfloat16).T)
-            row_dot = jnp.sum(go_f * out_t.astype(jnp.float32), axis=0, keepdims=True)
-            ds = (p * ((gp_t - row_dot) * (inv * scale))).astype(jnp.bfloat16)
-            dq_t = dot(keys_t[...], ds)
-            grad_k[...] += dot(ds, q)
-            ring[h, 0, here, :] = dq_t.astype(jnp.bfloat16).T
+            go_r = go_s.T
+
+            def probs_grad(c):
+                first, size = chunks[c]
+                return dot(values[pl.ds(first, size), :], go_s)
+
+            dq_t = 0.0
+            ahead = probs_grad(0)
+            for c, (first, size) in enumerate(chunks):
+                here_k = pl.ds(first, size)
+                gp_c = ahead
+                if c + 1 < len(chunks):
+                    ahead = probs_grad(c + 1)
+                grad_v[here_k, :] += dot(weights_b[c], go_r)
+                ds = weights_b[c] * (gp_c - row_dot).astype(jnp.bfloat16)
+                grad_k[here_k, :] += dot(ds, q)
+                dq_t = dq_t + dot(keys_t[:, here_k], ds)
+            ring[h, 0, here, :] = (dq_t * scale).astype(jnp.bfloat16).T
             ring[h, 3, here, :] = out_t.T
 
+        grad_k[...] = grad_k[...] * scale
         ring[h, 1] = grad_k[pl.ds(text, total_rows), :].astype(jnp.bfloat16)
         ring[h, 2] = grad_v[pl.ds(text, total_rows), :].astype(jnp.bfloat16)
         part = text // n
@@ -652,7 +680,7 @@
         and lax.axis_size("head") == 4
         and n % 2 == 0
         and rows % 64 == 0
-        and (rows * n) % 256 == 0
+        and (rows * n) % 512 == 0
         and rows * n <= 2048
         and depth % (128 * n) == 0
         and text_keys.shape[0] % (8 * n) == 0

time: 131 us -> 127 us (0.969)
  Pallas kernels: 123 us -> 119 us
    pallas_call x1, Pallas kernels: 123 us -> 119 us  [fused_device(): pl.pallas_call(functools.partial(fused_kernel, n, tile), out_shape=(jax.S...]
where the time goes in v3:
time: 127 us
  Pallas kernels  119 us (94%)
  other arithmetic  4.08 us (3%)
  local copies, waits for them, and re-layouts  2.88 us (2%)
    pallas_call x1, Pallas kernels, fused_device(): pl.pallas_call(functools.partial(fused_kernel, n, tile), out_shape=(jax.S...  119 us
    convert_element_type x1, other arithmetic, fused_device(): jnp.transpose(dwqkv, (1, 0, 2)).astype(f32)  2.54 us

profile of v3, /device:TPU:0, one launch (start us, length us, event | category | flops | bytes accessed | tf_op | source)
XLA Modules:
  0.0 126.7 jit_solution(2794356680014829116)
XLA Ops:
  0.6 0.7 compare_convert_fusion
  1.3 0.8 broadcast_in_dim.12.mask_ref
  2.1 119.0 %shard_map.110 = (bf16[192,768]{1,0:T(8,128)(2,1)}, bf16[3,384,384]{2,1,0:T(8,128)(2,1)}, bf16[384,384]{1,0:T(8,128)(2,1)}, f32[32,384]{1,0:T(8,128)}, f32[32,384]{1,0:T(8,128)}) custom-call(bf16[192,768]{1,0:T(8,128)(2,1)} %bitcast.16, bf16[192,768]{1,0:T(8,128)(2,1)} %bitcast.17, bf16[3,3072,384]{2,1,0:T(8,128)(2,1)} %bitcast.15, ...), custom_call_target="tpu_custom_call" | custom-call | flops 16307453952 | bytes 18874368 | tf_op jit(solution)/shard_map/pallas_call | solution.py:605
  121.2 0.0 copy-start
  121.2 0.0 copy-start.3
  121.2 0.0 copy-start.2
  121.2 0.0 copy-start.1
  121.2 2.5 %convert_bitcast_fusion = f32[384,3,384]{2,0,1:T(8,128)} fusion(bf16[3,384,384]{2,1,0:T(8,128)(2,1)} %get-tuple-element.11), kind=kLoop, calls=%fused_computation | loop fusion | flops 442368 | bytes 2654208 | tf_op jit(solution)/shard_map/convert_element_type | solution.py:667
  123.7 0.0 copy-done
  123.7 0.9 convert_element_type.12
  124.6 0.0 copy-done.3
  124.6 0.7 copy.12
  125.3 0.0 copy-done.2
  125.3 0.7 copy.13
  125.9 0.0 copy-done.1
  125.9 0.7 copy.15
Async XLA Ops:
  121.2 2.6 %copy-start = (bf16[384,384]{1,0:T(8,128)(2,1)S(1)}, bf16[384,384]{1,0:T(8,128)(2,1)}, u32[]{:S(2)}) copy-start(bf16[384,384]{1,0:T(8,128)(2,1)} %get-tuple-element.12) | copy-start | bytes 884740
  121.2 3.4 %copy-start.3 = (f32[32,384]{1,0:T(8,128)S(1)}, f32[32,384]{1,0:T(8,128)}, u32[]{:S(2)}) copy-start(f32[32,384]{1,0:T(8,128)} %get-tuple-element.13) | copy-start | bytes 147460
  121.2 4.1 %copy-start.2 = (f32[32,384]{1,0:T(8,128)S(1)}, f32[32,384]{1,0:T(8,128)}, u32[]{:S(2)}) copy-start(f32[32,384]{1,0:T(8,128)} %get-tuple-element.14) | copy-start | bytes 147460
  121.2 4.8 %copy-start.1 = (bf16[192,768]{1,0:T(8,128)(2,1)S(1)}, bf16[192,768]{1,0:T(8,128)(2,1)}, u32[]{:S(2)}) copy-start(bf16[192,768]{1,0:T(8,128)(2,1)} %get-tuple-element.10) | copy-start | bytes 884740

commit v4 on v3

--- a/solution.py
+++ b/solution.py
@@ -509,19 +509,19 @@
     hop(1, 0, 1)
     hop(0, 0, half)
     hop(0, 1, half)
+    early = [functools.partial(hop, 1, 0, s) for s in range(2, half + 1)]
+    early.insert(1, functools.partial(hop, 2, 0, 1))
+    early.append(functools.partial(hop, 2, 0, 2))
+    late = [functools.partial(hop, 2, 0, s) for s in range(3, half + 1)]
+    plan = [
+        [(e * tiles // len(early), run) for e, run in enumerate(early)],
+        [(e * tiles // (len(late) + 1), run) for e, run in enumerate(late)],
+        [(1, cols_start), (tiles - 1, cols_forward)],
+    ]
+    plan[1].append((plan[1][-1][0], swap_start))
     for h in range(heads):
         finish(h)
-        todo = []
-        if h + 1 < heads:
-            todo = [functools.partial(hop, h + 1, 0, s) for s in range(2, half + 1)]
-        if h + 2 < heads:
-            todo.insert(half - 2, functools.partial(hop, h + 2, 0, 1))
-        if h == 0:
-            todo.insert(0, swap_start)
-        if h == 1:
-            todo.insert(1, cols_start)
-            todo.append(cols_forward)
-        attend(h, [(e * tiles // len(todo), run) for e, run in enumerate(todo)])
+        attend(h, plan[h])
 
     for h in range(heads):
         for c in range(3):
@@ -683,6 +683,8 @@
         and (rows * n) % 512 == 0
         and rows * n <= 2048
         and depth % (128 * n) == 0
+        and qkv_weight.shape[2] == 3 * HD
+        and n >= 8
         and text_keys.shape[0] % (8 * n) == 0
     )
     chosen = fused_device if fits else plain_device

time: 127 us -> 117 us (0.921); the launches traced: 127 us -> 115 us
  Pallas kernels: 119 us -> 108 us
    pallas_call x1, Pallas kernels: 119 us -> 108 us  [fused_device(): pl.pallas_call(functools.partial(fused_kernel, n, tile), out_shape=(jax.S...]
where the time goes in v4:
time: 117 us; the launch traced here: 115 us
  Pallas kernels  108 us (92%)
  other arithmetic  4.08 us (3%)
  local copies, waits for them, and re-layouts  2.88 us (2%)
    pallas_call x1, Pallas kernels, fused_device(): pl.pallas_call(functools.partial(fused_kernel, n, tile), out_shape=(jax.S...  108 us
    convert_element_type x1, other arithmetic, fused_device(): jnp.transpose(dwqkv, (1, 0, 2)).astype(f32)  2.54 us

profile of v4, /device:TPU:0, one launch (start us, length us, event | category | flops | bytes accessed | tf_op | source)
XLA Modules:
  0.0 115.3 jit_solution(1242917972101455159)
XLA Ops:
  0.6 0.7 compare_convert_fusion
  1.3 0.8 broadcast_in_dim.12.mask_ref
  2.1 107.7 %shard_map.110 = (bf16[192,768]{1,0:T(8,128)(2,1)}, bf16[3,384,384]{2,1,0:T(8,128)(2,1)}, bf16[384,384]{1,0:T(8,128)(2,1)}, f32[32,384]{1,0:T(8,128)}, f32[32,384]{1,0:T(8,128)}) custom-call(bf16[192,768]{1,0:T(8,128)(2,1)} %bitcast.16, bf16[192,768]{1,0:T(8,128)(2,1)} %bitcast.17, bf16[3,3072,384]{2,1,0:T(8,128)(2,1)} %bitcast.15, ...), custom_call_target="tpu_custom_call" | custom-call | flops 16307453952 | bytes 18874368 | tf_op jit(solution)/shard_map/pallas_call | solution.py:605
  109.8 0.0 copy-start
  109.8 0.0 copy-start.3
  109.8 0.0 copy-start.2
  109.8 0.0 copy-start.1
  109.8 2.5 %convert_bitcast_fusion = f32[384,3,384]{2,0,1:T(8,128)} fusion(bf16[3,384,384]{2,1,0:T(8,128)(2,1)} %get-tuple-element.11), kind=kLoop, calls=%fused_computation | loop fusion | flops 442368 | bytes 2654208 | tf_op jit(solution)/shard_map/convert_element_type | solution.py:667
  112.4 0.0 copy-done
  112.4 0.9 convert_element_type.12
  113.2 0.0 copy-done.3
  113.2 0.7 copy.12
  113.9 0.0 copy-done.2
  113.9 0.7 copy.13
  114.6 0.0 copy-done.1
  114.6 0.7 copy.15
Async XLA Ops:
  109.8 2.6 %copy-start = (bf16[384,384]{1,0:T(8,128)(2,1)S(1)}, bf16[384,384]{1,0:T(8,128)(2,1)}, u32[]{:S(2)}) copy-start(bf16[384,384]{1,0:T(8,128)(2,1)} %get-tuple-element.12) | copy-start | bytes 884740
  109.8 3.4 %copy-start.3 = (f32[32,384]{1,0:T(8,128)S(1)}, f32[32,384]{1,0:T(8,128)}, u32[]{:S(2)}) copy-start(f32[32,384]{1,0:T(8,128)} %get-tuple-element.13) | copy-start | bytes 147460
  109.8 4.1 %copy-start.2 = (f32[32,384]{1,0:T(8,128)S(1)}, f32[32,384]{1,0:T(8,128)}, u32[]{:S(2)}) copy-start(f32[32,384]{1,0:T(8,128)} %get-tuple-element.14) | copy-start | bytes 147460
  109.8 4.8 %copy-start.1 = (bf16[192,768]{1,0:T(8,128)(2,1)S(1)}, bf16[192,768]{1,0:T(8,128)(2,1)}, u32[]{:S(2)}) copy-start(bf16[192,768]{1,0:T(8,128)(2,1)} %get-tuple-element.10) | copy-start | bytes 884740
